TPU v7x, 32 devices: a whole 2x2x4 slice. The times are simulated.
32 devices in a mesh: grp: 4 (over x, core), tp: 4 (over z), ex: 2 (over y).
Axes of the slice: x: 2, y: 2, z: 4, core: 2. Of those that a mesh axis runs over, the one named last changes fastest.
Arguments:
- tokens: bfloat16 [128, 7168], P(('grp', 'tp'), 'ex'), may hold values from -6 to 6
- expert_ids: int32 [128, 1], P(('grp', 'tp')), may hold values from 0 to 1; in each aligned block of 8 rows (0 to 7, 8 to 15, ...) at most 6 rows name the same one
- gate_levels: int32 [128, 1], P(('grp', 'tp')), may hold values from 1 to 4095
- gate_weight: bfloat16 [4, 7168, 1024], P('grp', 'ex', 'tp'), may hold values from -0.0625 to 0.0625
- up_weight: bfloat16 [4, 7168, 1024], P('grp', 'ex', 'tp'), may hold values from -0.0625 to 0.0625
- down_weight: bfloat16 [4, 1024, 7168], P('grp', 'tp', 'ex'), may hold values from -0.125 to 0.125
Outputs:
- mixed: bfloat16 [128, 7168], P(('grp', 'tp'), 'ex')
Inputs may be any that keep to these rules, and one draw needn't show every extreme that they name: `expert_ids`: each row names 1 different experts. In each aligned block of 8 rows (the tokens of one index pair of grp and tp) no expert is named by more than 6 rows.
All inputs are finite; a program needn't handle non-finite values.
Results may differ from a plain program's by a relative error of at most 0.0057.
Values may be sent and summed in bfloat16 or wider, within the bound.
No kernel may reach another device: no remote copies, remote signals or barrier semaphores. Data moves between devices by JAX's collectives and lax.ppermute only.
A program may use at most 64 MiB of HBM per device.

v0:
```python
import functools

import jax
import jax.numpy as jnp
from jax import lax
from jax.experimental import pallas as pl
from jax.experimental.pallas import tpu as pltpu
from jax.sharding import PartitionSpec as P

ROUTED_SCALE = 2.5
LANES = 128
MIB = 1024 * 1024


def shift(value, axis, by):
    size = lax.axis_size(axis)
    return lax.ppermute(value, axis, [(i, (i + by) % size) for i in range(size)])


def shift_expert(value, by):
    groups = lax.axis_size("grp")
    return lax.ppermute(value, "grp", [(i, (i + 2 * by) % groups) for i in range(groups)])


def swap_half(value):
    return lax.ppermute(value, "grp", [(i, i ^ 1) for i in range(lax.axis_size("grp"))])


def joined(parts):
    return parts[0] if len(parts) == 1 else jnp.concatenate(parts, axis=0)


def hand_on(*refs):
    del refs


def after(value, *earlier, flops=0):
    return pl.pallas_call(
        hand_on,
        out_shape=jax.ShapeDtypeStruct(value.shape, value.dtype),
        in_specs=[pl.BlockSpec(memory_space=pl.ANY)] * (1 + len(earlier)),
        out_specs=pl.BlockSpec(memory_space=pl.ANY),
        input_output_aliases={0: 0},
        cost_estimate=pl.CostEstimate(flops=flops, bytes_accessed=0, transcendentals=0),
        compiler_params=pltpu.CompilerParams(vmem_limit_bytes=MIB),
    )(value, *earlier)


def copy_kernel(from_ref, to_ref):
    to_ref[...] = from_ref[...]


def copied(value):
    return pl.pallas_call(
        copy_kernel,
        out_shape=jax.ShapeDtypeStruct(value.shape, value.dtype),
        compiler_params=pltpu.CompilerParams(vmem_limit_bytes=2 * MIB),
    )(value)


def weight_kernel(ids_ref, levels_ref, weight_ref):
    count = weight_ref.shape[0]
    top = ids_ref.shape[0]
    row = lax.broadcasted_iota(jnp.int32, (count, count), 0)
    column = lax.broadcasted_iota(jnp.int32, (count, count), 1)
    lane = lax.broadcasted_iota(jnp.int32, weight_ref.shape, 1)
    levels = levels_ref[...].astype(jnp.float32)
    shares = ROUTED_SCALE * levels / jnp.sum(levels, axis=0, keepdims=True)
    ids = ids_ref[...]
    weight = jnp.zeros(weight_ref.shape, jnp.float32)
    for j in range(top):
        chosen = jnp.sum(jnp.where(row == column, ids[j : j + 1, :], 0), axis=1, keepdims=True)
        share = jnp.sum(jnp.where(row == column, shares[j : j + 1, :], 0.0), axis=1, keepdims=True)
        weight = weight + jnp.where(lane == chosen, share, 0.0)
    weight_ref[...] = weight


def weights_of(expert_ids, gate_levels, experts):
    return pl.pallas_call(
        weight_kernel,
        out_shape=jax.ShapeDtypeStruct((expert_ids.shape[0], -(-experts // LANES) * LANES), jnp.float32),
        compiler_params=pltpu.CompilerParams(vmem_limit_bytes=MIB),
    )(expert_ids.T, gate_levels.T)


def blend_kernel(experts, start, blocks, near_ref, *refs):
    weight_refs, far_refs, out_refs = refs[:blocks], refs[blocks : blocks + experts - 1], refs[blocks + experts - 1 :]
    expert = lax.axis_index("grp") // 2
    count = out_refs[0].shape[0]
    for i in range(blocks):
        weight = weight_refs[i][...]
        lane = lax.broadcasted_iota(jnp.int32, weight.shape, 1)
        mixed = jnp.zeros(out_refs[i].shape, jnp.float32)
        for s in range(experts):
            source = lax.rem(expert + s, experts)
            column = jnp.sum(jnp.where(lane == source, weight, 0.0), axis=1, keepdims=True)
            if s:
                rows = far_refs[s - 1][i * count : (i + 1) * count, :].astype(jnp.float32)
            else:
                rows = near_ref[start + i * count : start + (i + 1) * count, :]
            mixed = mixed + column * rows
        out_refs[i][...] = mixed.astype(out_refs[i].dtype)


def blended(near, start, weights, fars, types):
    count, width = weights[0].shape[0], near.shape[1]
    return pl.pallas_call(
        functools.partial(blend_kernel, len(fars) + 1, start, len(weights)),
        out_shape=[jax.ShapeDtypeStruct((count, width), kind) for kind in types],
        compiler_params=pltpu.CompilerParams(vmem_limit_bytes=16 * MIB),
    )(near, *weights, *fars)


def per_device(tokens, expert_ids, gate_levels, gate_weight, up_weight, down_weight):
    bf16, f32 = jnp.bfloat16, jnp.float32
    experts = lax.axis_size("grp") // 2
    n_tp, n_ex = lax.axis_size("tp"), lax.axis_size("ex")
    count, width = tokens.shape
    w_gate, w_up, w_down = gate_weight[0], up_weight[0], down_weight[0]
    inner = w_down.shape[0]
    others = range(1, experts)

    def partial_sums(rows):
        part = jnp.concatenate([jnp.dot(rows, w, preferred_element_type=f32) for w in (w_gate, w_up)], axis=1)
        sent = part.astype(bf16)
        return part, sent, [shift(sent, "ex", s) for s in range(1, n_ex)]

    def partial_out(part, others, part_flops, kept_flops):
        if part_flops:
            part = after(part, flops=part_flops)
        for other in others:
            part = part + other.astype(f32)
        hidden = (jax.nn.silu(part[:, :inner]) * part[:, inner:]).astype(bf16)
        out = jnp.dot(hidden, w_down, preferred_element_type=f32)
        kept = out.shape[0] // 2
        swapped = swap_half(out[kept:].astype(bf16)).astype(f32)
        if kept_flops:
            out = after(out, flops=kept_flops)
        return out[:kept] + swapped

    held = copied(tokens)
    places = tuple(range(1, n_tp))
    rest = joined([shift(tokens, "tp", t) for t in places])
    far_own = [shift_expert(held, s) for s in others]
    far_rest = [shift_expert(rest, s) for s in others]
    near = joined([held, rest])
    near_swapped = swap_half(near)
    near = joined([near, near_swapped])
    near_part, near_sent, near_others = partial_sums(near)
    far = joined([rows for own, other in zip(far_own, far_rest) for rows in (own, after(other, near_sent))])
    far_swapped = swap_half(far)
    far = joined([after(far, flops=3450000000), far_swapped])
    far_part, far_sent, far_others = partial_sums(far)
    near_out = partial_out(near_part, [after(other, far_sent) for other in near_others], 3450000000, 3450000000)
    far_out = partial_out(far_part, [after(other, near_out) for other in far_others], 0, 0).astype(bf16)
    own_weight = weights_of(expert_ids, gate_levels, experts)
    weights = [shift(own_weight, "tp", t) for t in places]
    line, half = n_tp * count, 2 * count
    back_b = [shift_expert(far_out[(s - 1) * line + half : s * line], -s) for s in others]
    back_a = [shift_expert(far_out[(s - 1) * line : (s - 1) * line + half], -s) for s in others]
    pieces_b = blended(near_out, half, weights[1:], back_b, [bf16] * (n_tp - 2))
    own, piece_a = blended(near_out, 0, [own_weight, weights[0]], back_a, [f32, bf16])
    mixed = own
    for t, piece in zip(places, [piece_a, *pieces_b]):
        mixed = mixed + shift(piece, "tp", -t).astype(f32)
    return mixed.astype(bf16)


def solution(mesh):
    return jax.shard_map(
        per_device,
        mesh=mesh,
        in_specs=(
            P(("grp", "tp"), "ex"),
            P(("grp", "tp"), None),
            P(("grp", "tp"), None),
            P("grp", "ex", "tp"),
            P("grp", "ex", "tp"),
            P("grp", "tp", "ex"),
        ),
        out_specs=P(("grp", "tp"), "ex"),
        check_vma=False,
    )
```

profile of v0, /device:TPU:0, one launch (start us, length us, event | category | flops | bytes accessed | tf_op | source)
XLA Modules:
  0.0 43.4 jit_solution(7367892640080580395)
XLA Ops:
  0.0 0.0 copy-start
  0.0 3.0 %collective-permute-start = (bf16[8,3584]{1,0:T(8,128)(2,1)}, bf16[8,3584]{1,0:T(8,128)(2,1)S(1)}, u32[]{:S(2)}, u32[]{:S(2)}) collective-permute-start(bf16[8,3584]{1,0:T(8,128)(2,1)} %from_ref.1), channel_id=1, source_target_pairs={{0,2},{2,4},{4,6},{6,0},{1,3},{3,5},{5,7},{7,1},{8,10},{10,12},{12... | collective-permute-start | bytes 172040 | tf_op jit(solution)/shard_map/ppermute | solution.py:17
  3.0 2.6 %collective-permute-start.1 = (bf16[8,3584]{1,0:T(8,128)(2,1)}, bf16[8,3584]{1,0:T(8,128)(2,1)S(1)}, u32[]{:S(2)}, u32[]{:S(2)}) collective-permute-start(bf16[8,3584]{1,0:T(8,128)(2,1)} %from_ref.1), channel_id=1, source_target_pairs={{0,4},{2,6},{4,0},{6,2},{1,5},{3,7},{5,1},{7,3},{8,12},{10,14},{12... | collective-permute-start | bytes 172040 | tf_op jit(solution)/shard_map/ppermute | solution.py:17
  5.6 1.3 %collective-permute-start.2 = (bf16[8,3584]{1,0:T(8,128)(2,1)}, bf16[8,3584]{1,0:T(8,128)(2,1)S(1)}, u32[]{:S(2)}, u32[]{:S(2)}) collective-permute-start(bf16[8,3584]{1,0:T(8,128)(2,1)} %from_ref.1), channel_id=1, source_target_pairs={{0,6},{2,0},{4,2},{6,4},{1,7},{3,1},{5,3},{7,5},{8,14},{10,8},{12,... | collective-permute-start | bytes 172040 | tf_op jit(solution)/shard_map/ppermute | solution.py:17
  7.0 0.0 copy-start.1
  7.0 0.9 %copy-done.1 = bf16[8,3584]{1,0:T(8,128)(2,1)S(1)} copy-done((bf16[8,3584]{1,0:T(8,128)(2,1)S(1)}, bf16[8,3584]{1,0:T(8,128)(2,1)}, u32[]{:S(2)}) %copy-start.1) | copy-done | bytes 57368
  7.8 1.5 %collective-permute-start.5 = (bf16[8,3584]{1,0:T(8,128)(2,1)S(1)}, bf16[8,3584]{1,0:T(8,128)(2,1)S(1)}, u32[]{:S(2)}, u32[]{:S(2)}) collective-permute-start(bf16[8,3584]{1,0:T(8,128)(2,1)S(1)} %shard_map.64), channel_id=1, source_target_pairs={{0,16},{8,24},{16,0},{24,8},{1,17},{9,25},{17,1},{25,9},{2,18},{10... | collective-permute-start | bytes 172040 | tf_op jit(solution)/shard_map/ppermute | solution.py:22
  9.3 0.0 collective-permute-done
  9.3 0.5 %collective-permute-done.1 = bf16[8,3584]{1,0:T(8,128)(2,1)S(1)} collective-permute-done((bf16[8,3584]{1,0:T(8,128)(2,1)}, bf16[8,3584]{1,0:T(8,128)(2,1)S(1)}, u32[]{:S(2)}, u32[]{:S(2)}) %collective-permute-start.1) | collective-permute-done | bytes 57376 | tf_op jit(solution)/shard_map/ppermute | solution.py:17
  9.9 0.4 collective-permute-done.2
  10.2 0.0 copy-start.5
  10.3 0.1 collective-permute-start.3
  10.4 1.6 %collective-permute-start.6 = (bf16[24,3584]{1,0:T(8,128)(2,1)S(1)}, bf16[24,3584]{1,0:T(8,128)(2,1)S(1)}, u32[]{:S(2)}, u32[]{:S(2)}) collective-permute-start(bf16[24,3584]{1,0:T(8,128)(2,1)S(1)} %pad_maximum_fusion.5), channel_id=1, source_target_pairs={{0,16},{8,24},{16,0},{24,8},{1,17},{9,25},{17,1},{25,9},{2,18},{10... | collective-permute-start | bytes 516104 | tf_op jit(solution)/shard_map/ppermute | solution.py:22
  12.0 0.0 collective-permute-done.3
  12.0 1.9 %fusion.10 = f32[64,256]{1,0:T(8,128)S(1)} fusion(bf16[64,3584]{1,0:T(8,128)(2,1)S(1)} %constant_dynamic-update-slice_fusion, bf16[1,3584,256]{2,1,0:T(8,128)(2,1)} %param.9), kind=kOutput, calls=%fused_computation.10 | convolution fusion | flops 117440512 | bytes 2359296 | tf_op jit(solution)/shard_map/dot_general | solution.py:124
  14.0 0.0 copy-done.5
  14.0 0.4 %fusion.6 = f32[64,256]{1,0:T(8,128)S(1)} fusion(bf16[64,3584]{1,0:T(8,128)(2,1)S(1)} %constant_dynamic-update-slice_fusion, bf16[1,3584,256]{2,1,0:T(8,128)(2,1)S(1)} %copy-done.5), kind=kOutput, calls=%fused_computation.6 | convolution fusion | flops 117440512 | bytes 2359296 | tf_op jit(solution)/shard_map/dot_general | solution.py:124
  14.5 1.6 %collective-permute-start.4 = (bf16[64,512]{1,0:T(8,128)(2,1)S(1)}, bf16[64,512]{1,0:T(8,128)(2,1)S(1)}, u32[]{:S(2)}, u32[]{:S(2)}) collective-permute-start(bf16[64,512]{1,0:T(8,128)(2,1)S(1)} %fusion.24.refs_1_), channel_id=1, source_target_pairs={{0,1},{1,0},{2,3},{3,2},{4,5},{5,4},{6,7},{7,6},{8,9},{9,8},{10,11... | collective-permute-start | bytes 196616 | tf_op jit(solution)/shard_map/ppermute | solution.py:17
  16.1 1.1 %collective-permute-done.6.refs_0_ = bf16[24,3584]{1,0:T(8,128)(2,1)S(1)} collective-permute-done((bf16[24,3584]{1,0:T(8,128)(2,1)S(1)}, bf16[24,3584]{1,0:T(8,128)(2,1)S(1)}, u32[]{:S(2)}, u32[]{:S(2)}) %collective-permute-start.6) | collective-permute-done | bytes 172064 | tf_op jit(solution)/shard_map/ppermute | solution.py:22
  17.2 0.0 collective-permute-done.5
  17.2 0.1 collective-permute-start.7
  17.3 0.0 copy-start.4
  17.3 1.5 %collective-permute-done.7 = bf16[32,3584]{1,0:T(8,128)(2,1)S(1)} collective-permute-done((bf16[32,3584]{1,0:T(8,128)(2,1)S(1)}, bf16[32,3584]{1,0:T(8,128)(2,1)S(1)}, u32[]{:S(2)}, u32[]{:S(2)}) %collective-permute-start.7) | collective-permute-done | bytes 229408 | tf_op jit(solution)/shard_map/ppermute | solution.py:26
  18.8 0.0 copy-done.4
  18.8 0.4 %fusion.8 = f32[64,256]{1,0:T(8,128)S(1)} fusion(bf16[1,3584,256]{2,1,0:T(8,128)(2,1)S(1)} %copy-done.4, bf16[32,3584]{1,0:T(8,128)(2,1)S(1)} %collective-permute-done.7, bf16[32,3584]{1,0:T(8,128)(2,1)S(1)} %shard_map.67), kind=kOutput, calls=%fused_computation.8 | convolution fusion | flops 118358016 | bytes 2359296 | tf_op jit(solution)/shard_map/dot_general | solution.py:124
  19.2 0.4 %fusion.4 = f32[64,256]{1,0:T(8,128)S(1)} fusion(bf16[1,3584,256]{2,1,0:T(8,128)(2,1)S(1)} %copy-done.5, bf16[32,3584]{1,0:T(8,128)(2,1)S(1)} %collective-permute-done.7, bf16[32,3584]{1,0:T(8,128)(2,1)S(1)} %shard_map.67), kind=kOutput, calls=%fused_computation.4 | convolution fusion | flops 118358016 | bytes 2359296 | tf_op jit(solution)/shard_map/dot_general | solution.py:124
  19.7 1.7 %collective-permute-start.10 = (bf16[64,512]{1,0:T(8,128)(2,1)S(1)}, bf16[64,512]{1,0:T(8,128)(2,1)S(1)}, u32[]{:S(2)}, u32[]{:S(2)}) collective-permute-start(bf16[64,512]{1,0:T(8,128)(2,1)S(1)} %fusion.13.refs_1_), channel_id=1, source_target_pairs={{0,1},{1,0},{2,3},{3,2},{4,5},{5,4},{6,7},{7,6},{8,9},{9,8},{10,11... | collective-permute-start | bytes 196616 | tf_op jit(solution)/shard_map/ppermute | solution.py:17
  21.4 0.0 collective-permute-done.4.refs_0_
  21.4 0.0 copy-done
  21.4 0.4 fusion.2.refs_0_
  21.9 0.3 collective-permute-start.8
  22.1 1.3 %collective-permute-done.8 = bf16[32,3584]{1,0:T(8,128)(2,1)S(1)} collective-permute-done((bf16[32,3584]{1,0:T(8,128)(2,1)S(1)}, bf16[32,3584]{1,0:T(8,128)(2,1)S(1)}, u32[]{:S(2)}, u32[]{:S(2)}) %collective-permute-start.8) | collective-permute-done | bytes 229408 | tf_op jit(solution)/shard_map/ppermute | solution.py:26
  23.4 0.8 %collective-permute-done.10.refs_0_ = bf16[64,512]{1,0:T(8,128)(2,1)S(1)} collective-permute-done((bf16[64,512]{1,0:T(8,128)(2,1)S(1)}, bf16[64,512]{1,0:T(8,128)(2,1)S(1)}, u32[]{:S(2)}, u32[]{:S(2)}) %collective-permute-start.10) | collective-permute-done | bytes 65568 | tf_op jit(solution)/shard_map/ppermute | solution.py:17
  24.3 0.0 copy-start.2
  24.3 0.0 copy-start.3
  24.3 0.4 fusion
  24.8 0.1 collective-permute-start.11
  24.8 1.5 %collective-permute-done.11 = bf16[32,3584]{1,0:T(8,128)(2,1)S(1)} collective-permute-done((bf16[32,3584]{1,0:T(8,128)(2,1)S(1)}, bf16[32,3584]{1,0:T(8,128)(2,1)S(1)}, u32[]{:S(2)}, u32[]{:S(2)}) %collective-permute-start.11) | collective-permute-done | bytes 229408 | tf_op jit(solution)/shard_map/ppermute | solution.py:26
  26.3 0.1 fusion.12
  26.4 1.6 %collective-permute-start.12 = (bf16[16,3584]{1,0:T(8,128)(2,1)S(1)}, bf16[16,3584]{1,0:T(8,128)(2,1)S(1)}, u32[]{:S(2)}, u32[]{:S(2)}) collective-permute-start(bf16[16,3584]{1,0:T(8,128)(2,1)S(1)} %get-tuple-element.13), channel_id=1, source_target_pairs={{0,16},{8,24},{16,0},{24,8},{1,17},{9,25},{17,1},{25,9},{2,18},{10... | collective-permute-start | bytes 344072 | tf_op jit(solution)/shard_map/ppermute | solution.py:22
  28.0 0.5 %collective-permute-start.16 = (bf16[16,3584]{1,0:T(8,128)(2,1)S(1)}, bf16[16,3584]{1,0:T(8,128)(2,1)S(1)}, u32[]{:S(2)}, u32[]{:S(2)}) collective-permute-start(bf16[16,3584]{1,0:T(8,128)(2,1)S(1)} %get-tuple-element.14), channel_id=1, source_target_pairs={{0,16},{8,24},{16,0},{24,8},{1,17},{9,25},{17,1},{25,9},{2,18},{10... | collective-permute-start | bytes 344072 | tf_op jit(solution)/shard_map/ppermute | solution.py:22
  28.5 0.0 copy-done.2
  28.5 0.0 copy-done.3
  28.5 0.1 shard_map.70.refs_0_
  28.6 1.2 %collective-permute-start.9 = (f32[8,128]{1,0:T(8,128)S(1)}, f32[8,128]{1,0:T(8,128)S(1)}, u32[]{:S(2)}, u32[]{:S(2)}) collective-permute-start(f32[8,128]{1,0:T(8,128)S(1)} %shard_map.70.refs_0_), channel_id=1, source_target_pairs={{0,2},{2,4},{4,6},{6,0},{1,3},{3,5},{5,7},{7,1},{8,10},{10,12},{12... | collective-permute-start | bytes 12296 | tf_op jit(solution)/shard_map/ppermute | solution.py:17
  29.8 2.3 %collective-permute-start.14 = (f32[8,128]{1,0:T(8,128)S(1)}, f32[8,128]{1,0:T(8,128)S(1)}, u32[]{:S(2)}, u32[]{:S(2)}) collective-permute-start(f32[8,128]{1,0:T(8,128)S(1)} %shard_map.70.refs_0_), channel_id=1, source_target_pairs={{0,4},{2,6},{4,0},{6,2},{1,5},{3,7},{5,1},{7,3},{8,12},{10,14},{12... | collective-permute-start | bytes 12296 | tf_op jit(solution)/shard_map/ppermute | solution.py:17
  32.1 0.4 collective-permute-start.15
  32.5 1.5 %collective-permute-done.9.refs_1_ = f32[8,128]{1,0:T(8,128)S(1)} collective-permute-done((f32[8,128]{1,0:T(8,128)S(1)}, f32[8,128]{1,0:T(8,128)S(1)}, u32[]{:S(2)}, u32[]{:S(2)}) %collective-permute-start.9) | collective-permute-done | bytes 4128 | tf_op jit(solution)/shard_map/ppermute | solution.py:17
  34.0 0.0 collective-permute-done.12.refs_2_
  34.0 0.1 shard_map.72
  34.1 1.4 %collective-permute-start.13 = (bf16[8,3584]{1,0:T(8,128)(2,1)S(1)}, bf16[8,3584]{1,0:T(8,128)(2,1)S(1)}, u32[]{:S(2)}, u32[]{:S(2)}) collective-permute-start(bf16[8,3584]{1,0:T(8,128)(2,1)S(1)} %get-tuple-element.10), channel_id=1, source_target_pairs={{0,6},{2,0},{4,2},{6,4},{1,7},{3,1},{5,3},{7,5},{8,14},{10,8},{12,... | collective-permute-start | bytes 172040 | tf_op jit(solution)/shard_map/ppermute | solution.py:17
  35.6 0.0 collective-permute-done.14.refs_0_
  35.6 0.1 collective-permute-done.15.refs_1_
  35.7 0.0 collective-permute-done.16.refs_2_
  35.7 0.1 shard_map.73
  35.8 1.0 %collective-permute-start.17 = (bf16[8,3584]{1,0:T(8,128)(2,1)S(1)}, bf16[8,3584]{1,0:T(8,128)(2,1)S(1)}, u32[]{:S(2)}, u32[]{:S(2)}) collective-permute-start(bf16[8,3584]{1,0:T(8,128)(2,1)S(1)} %get-tuple-element.11), channel_id=1, source_target_pairs={{0,4},{2,6},{4,0},{6,2},{1,5},{3,7},{5,1},{7,3},{8,12},{10,14},{12... | collective-permute-start | bytes 172040 | tf_op jit(solution)/shard_map/ppermute | solution.py:17
  36.8 1.8 %collective-permute-start.18 = (bf16[8,3584]{1,0:T(8,128)(2,1)S(1)}, bf16[8,3584]{1,0:T(8,128)(2,1)S(1)}, u32[]{:S(2)}, u32[]{:S(2)}) collective-permute-start(bf16[8,3584]{1,0:T(8,128)(2,1)S(1)} %get-tuple-element.12), channel_id=1, source_target_pairs={{0,2},{2,4},{4,6},{6,0},{1,3},{3,5},{5,7},{7,1},{8,10},{10,12},{12... | collective-permute-start | bytes 172040 | tf_op jit(solution)/shard_map/ppermute | solution.py:17
  38.6 0.0 collective-permute-done.13
  38.6 2.9 %collective-permute-done.17 = bf16[8,3584]{1,0:T(8,128)(2,1)S(1)} collective-permute-done((bf16[8,3584]{1,0:T(8,128)(2,1)S(1)}, bf16[8,3584]{1,0:T(8,128)(2,1)S(1)}, u32[]{:S(2)}, u32[]{:S(2)}) %collective-permute-start.17) | collective-permute-done | bytes 57376 | tf_op jit(solution)/shard_map/ppermute | solution.py:17
  41.6 1.2 %collective-permute-done.18 = bf16[8,3584]{1,0:T(8,128)(2,1)S(1)} collective-permute-done((bf16[8,3584]{1,0:T(8,128)(2,1)S(1)}, bf16[8,3584]{1,0:T(8,128)(2,1)S(1)}, u32[]{:S(2)}, u32[]{:S(2)}) %collective-permute-start.18) | collective-permute-done | bytes 57376 | tf_op jit(solution)/shard_map/ppermute | solution.py:17
  42.8 0.7 %add_convert_fusion = bf16[8,3584]{1,0:T(8,128)(2,1)} fusion(bf16[8,3584]{1,0:T(8,128)(2,1)S(1)} %collective-permute-done.18, bf16[8,3584]{1,0:T(8,128)(2,1)S(1)} %collective-permute-done.17, f32[8,3584]{1,0:T(8,128)S(1)} %get-tuple-element.9, bf16[8,3584]{1,0:T(8,128)(2,1)S(1)} %collective-permute-done.13), kind=kLoop, calls=%fused_computation.25 | loop fusion | flops 200704 | bytes 344064 | tf_op jit(solution)/shard_map/convert_element_type | solution.py:166
  (24 shorter events, 0.3 us)
Async XLA Ops:
  0.0 21.4 %copy-start = (bf16[1,256,3584]{2,1,0:T(8,128)(2,1)S(1)}, bf16[1,256,3584]{2,1,0:T(8,128)(2,1)}, u32[]{:S(2)}) copy-start(bf16[1,256,3584]{2,1,0:T(8,128)(2,1)} %param.11) | copy-start | bytes 5505028
  0.0 9.3 %collective-permute-start = (bf16[8,3584]{1,0:T(8,128)(2,1)}, bf16[8,3584]{1,0:T(8,128)(2,1)S(1)}, u32[]{:S(2)}, u32[]{:S(2)}) collective-permute-start(bf16[8,3584]{1,0:T(8,128)(2,1)} %from_ref.1), channel_id=1, source_target_pairs={{0,2},{2,4},{4,6},{6,0},{1,3},{3,5},{5,7},{7,1},{8,10},{10,12},{12... | collective-permute-start | bytes 172040 | tf_op jit(solution)/shard_map/ppermute | solution.py:17
  3.0 6.8 %collective-permute-start.1 = (bf16[8,3584]{1,0:T(8,128)(2,1)}, bf16[8,3584]{1,0:T(8,128)(2,1)S(1)}, u32[]{:S(2)}, u32[]{:S(2)}) collective-permute-start(bf16[8,3584]{1,0:T(8,128)(2,1)} %from_ref.1), channel_id=1, source_target_pairs={{0,4},{2,6},{4,0},{6,2},{1,5},{3,7},{5,1},{7,3},{8,12},{10,14},{12... | collective-permute-start | bytes 172040 | tf_op jit(solution)/shard_map/ppermute | solution.py:17
  5.6 4.6 %collective-permute-start.2 = (bf16[8,3584]{1,0:T(8,128)(2,1)}, bf16[8,3584]{1,0:T(8,128)(2,1)S(1)}, u32[]{:S(2)}, u32[]{:S(2)}) collective-permute-start(bf16[8,3584]{1,0:T(8,128)(2,1)} %from_ref.1), channel_id=1, source_target_pairs={{0,6},{2,0},{4,2},{6,4},{1,7},{3,1},{5,3},{7,5},{8,14},{10,8},{12,... | collective-permute-start | bytes 172040 | tf_op jit(solution)/shard_map/ppermute | solution.py:17
  7.0 0.9 %copy-start.1 = (bf16[8,3584]{1,0:T(8,128)(2,1)S(1)}, bf16[8,3584]{1,0:T(8,128)(2,1)}, u32[]{:S(2)}) copy-start(bf16[8,3584]{1,0:T(8,128)(2,1)} %from_ref.1) | copy-start | bytes 172036
  7.8 9.4 %collective-permute-start.5 = (bf16[8,3584]{1,0:T(8,128)(2,1)S(1)}, bf16[8,3584]{1,0:T(8,128)(2,1)S(1)}, u32[]{:S(2)}, u32[]{:S(2)}) collective-permute-start(bf16[8,3584]{1,0:T(8,128)(2,1)S(1)} %shard_map.64), channel_id=1, source_target_pairs={{0,16},{8,24},{16,0},{24,8},{1,17},{9,25},{17,1},{25,9},{2,18},{10... | collective-permute-start | bytes 172040 | tf_op jit(solution)/shard_map/ppermute | solution.py:22
  10.2 3.7 %copy-start.5 = (bf16[1,3584,256]{2,1,0:T(8,128)(2,1)S(1)}, bf16[1,3584,256]{2,1,0:T(8,128)(2,1)}, u32[]{:S(2)}) copy-start(bf16[1,3584,256]{2,1,0:T(8,128)(2,1)} %param.10) | copy-start | bytes 5505028
  10.3 1.8 %collective-permute-start.3 = (bf16[32,3584]{1,0:T(8,128)(2,1)S(1)}, bf16[32,3584]{1,0:T(8,128)(2,1)S(1)}, u32[]{:S(2)}, u32[]{:S(2)}) collective-permute-start(bf16[32,3584]{1,0:T(8,128)(2,1)S(1)} %pad_maximum_fusion.3), channel_id=1, source_target_pairs={{0,8},{8,0},{16,24},{24,16},{1,9},{9,1},{17,25},{25,17},{2,10},{10... | collective-permute-start | bytes 688136 | tf_op jit(solution)/shard_map/ppermute | solution.py:26
  10.4 6.8 %collective-permute-start.6 = (bf16[24,3584]{1,0:T(8,128)(2,1)S(1)}, bf16[24,3584]{1,0:T(8,128)(2,1)S(1)}, u32[]{:S(2)}, u32[]{:S(2)}) collective-permute-start(bf16[24,3584]{1,0:T(8,128)(2,1)S(1)} %pad_maximum_fusion.5), channel_id=1, source_target_pairs={{0,16},{8,24},{16,0},{24,8},{1,17},{9,25},{17,1},{25,9},{2,18},{10... | collective-permute-start | bytes 516104 | tf_op jit(solution)/shard_map/ppermute | solution.py:22
  14.5 6.9 %collective-permute-start.4 = (bf16[64,512]{1,0:T(8,128)(2,1)S(1)}, bf16[64,512]{1,0:T(8,128)(2,1)S(1)}, u32[]{:S(2)}, u32[]{:S(2)}) collective-permute-start(bf16[64,512]{1,0:T(8,128)(2,1)S(1)} %fusion.24.refs_1_), channel_id=1, source_target_pairs={{0,1},{1,0},{2,3},{3,2},{4,5},{5,4},{6,7},{7,6},{8,9},{9,8},{10,11... | collective-permute-start | bytes 196616 | tf_op jit(solution)/shard_map/ppermute | solution.py:17
  17.2 1.6 %collective-permute-start.7 = (bf16[32,3584]{1,0:T(8,128)(2,1)S(1)}, bf16[32,3584]{1,0:T(8,128)(2,1)S(1)}, u32[]{:S(2)}, u32[]{:S(2)}) collective-permute-start(bf16[32,3584]{1,0:T(8,128)(2,1)S(1)} %pad_maximum_fusion.4.refs_0_), channel_id=1, source_target_pairs={{0,8},{8,0},{16,24},{24,16},{1,9},{9,1},{17,25},{25,17},{2,10},{10... | collective-permute-start | bytes 688136 | tf_op jit(solution)/shard_map/ppermute | solution.py:26
  17.3 1.5 %copy-start.4 = (bf16[1,3584,256]{2,1,0:T(8,128)(2,1)S(1)}, bf16[1,3584,256]{2,1,0:T(8,128)(2,1)}, u32[]{:S(2)}) copy-start(bf16[1,3584,256]{2,1,0:T(8,128)(2,1)} %param.9) | copy-start | bytes 5505028
  19.7 4.5 %collective-permute-start.10 = (bf16[64,512]{1,0:T(8,128)(2,1)S(1)}, bf16[64,512]{1,0:T(8,128)(2,1)S(1)}, u32[]{:S(2)}, u32[]{:S(2)}) collective-permute-start(bf16[64,512]{1,0:T(8,128)(2,1)S(1)} %fusion.13.refs_1_), channel_id=1, source_target_pairs={{0,1},{1,0},{2,3},{3,2},{4,5},{5,4},{6,7},{7,6},{8,9},{9,8},{10,11... | collective-permute-start | bytes 196616 | tf_op jit(solution)/shard_map/ppermute | solution.py:17
  21.9 1.6 %collective-permute-start.8 = (bf16[32,3584]{1,0:T(8,128)(2,1)S(1)}, bf16[32,3584]{1,0:T(8,128)(2,1)S(1)}, u32[]{:S(2)}, u32[]{:S(2)}) collective-permute-start(bf16[32,3584]{1,0:T(8,128)(2,1)S(1)} %slice.71), channel_id=1, source_target_pairs={{0,8},{8,0},{16,24},{24,16},{1,9},{9,1},{17,25},{25,17},{2,10},{10... | collective-permute-start | bytes 688136 | tf_op jit(solution)/shard_map/ppermute | solution.py:26
  24.3 4.2 %copy-start.2 = (s32[8,1]{0,1:T(1,128)S(1)}, s32[8,1]{0,1:T(1,128)}, u32[]{:S(2)}) copy-start(s32[8,1]{0,1:T(1,128)} %param.7) | copy-start | bytes 100
  24.3 4.2 %copy-start.3 = (s32[8,1]{0,1:T(1,128)S(1)}, s32[8,1]{0,1:T(1,128)}, u32[]{:S(2)}) copy-start(s32[8,1]{0,1:T(1,128)} %param.8) | copy-start | bytes 100
  24.8 1.6 %collective-permute-start.11 = (bf16[32,3584]{1,0:T(8,128)(2,1)S(1)}, bf16[32,3584]{1,0:T(8,128)(2,1)S(1)}, u32[]{:S(2)}, u32[]{:S(2)}) collective-permute-start(bf16[32,3584]{1,0:T(8,128)(2,1)S(1)} %slice.70), channel_id=1, source_target_pairs={{0,8},{8,0},{16,24},{24,16},{1,9},{9,1},{17,25},{25,17},{2,10},{10... | collective-permute-start | bytes 688136 | tf_op jit(solution)/shard_map/ppermute | solution.py:26
  26.4 7.6 %collective-permute-start.12 = (bf16[16,3584]{1,0:T(8,128)(2,1)S(1)}, bf16[16,3584]{1,0:T(8,128)(2,1)S(1)}, u32[]{:S(2)}, u32[]{:S(2)}) collective-permute-start(bf16[16,3584]{1,0:T(8,128)(2,1)S(1)} %get-tuple-element.13), channel_id=1, source_target_pairs={{0,16},{8,24},{16,0},{24,8},{1,17},{9,25},{17,1},{25,9},{2,18},{10... | collective-permute-start | bytes 344072 | tf_op jit(solution)/shard_map/ppermute | solution.py:22
  28.0 7.7 %collective-permute-start.16 = (bf16[16,3584]{1,0:T(8,128)(2,1)S(1)}, bf16[16,3584]{1,0:T(8,128)(2,1)S(1)}, u32[]{:S(2)}, u32[]{:S(2)}) collective-permute-start(bf16[16,3584]{1,0:T(8,128)(2,1)S(1)} %get-tuple-element.14), channel_id=1, source_target_pairs={{0,16},{8,24},{16,0},{24,8},{1,17},{9,25},{17,1},{25,9},{2,18},{10... | collective-permute-start | bytes 344072 | tf_op jit(solution)/shard_map/ppermute | solution.py:22
  28.6 5.4 %collective-permute-start.9 = (f32[8,128]{1,0:T(8,128)S(1)}, f32[8,128]{1,0:T(8,128)S(1)}, u32[]{:S(2)}, u32[]{:S(2)}) collective-permute-start(f32[8,128]{1,0:T(8,128)S(1)} %shard_map.70.refs_0_), channel_id=1, source_target_pairs={{0,2},{2,4},{4,6},{6,0},{1,3},{3,5},{5,7},{7,1},{8,10},{10,12},{12... | collective-permute-start | bytes 12296 | tf_op jit(solution)/shard_map/ppermute | solution.py:17
  29.8 5.8 %collective-permute-start.14 = (f32[8,128]{1,0:T(8,128)S(1)}, f32[8,128]{1,0:T(8,128)S(1)}, u32[]{:S(2)}, u32[]{:S(2)}) collective-permute-start(f32[8,128]{1,0:T(8,128)S(1)} %shard_map.70.refs_0_), channel_id=1, source_target_pairs={{0,4},{2,6},{4,0},{6,2},{1,5},{3,7},{5,1},{7,3},{8,12},{10,14},{12... | collective-permute-start | bytes 12296 | tf_op jit(solution)/shard_map/ppermute | solution.py:17
  32.1 3.6 %collective-permute-start.15 = (f32[8,128]{1,0:T(8,128)S(1)}, f32[8,128]{1,0:T(8,128)S(1)}, u32[]{:S(2)}, u32[]{:S(2)}) collective-permute-start(f32[8,128]{1,0:T(8,128)S(1)} %shard_map.70.refs_0_), channel_id=1, source_target_pairs={{0,6},{2,0},{4,2},{6,4},{1,7},{3,1},{5,3},{7,5},{8,14},{10,8},{12,... | collective-permute-start | bytes 12296 | tf_op jit(solution)/shard_map/ppermute | solution.py:17
  34.1 4.5 %collective-permute-start.13 = (bf16[8,3584]{1,0:T(8,128)(2,1)S(1)}, bf16[8,3584]{1,0:T(8,128)(2,1)S(1)}, u32[]{:S(2)}, u32[]{:S(2)}) collective-permute-start(bf16[8,3584]{1,0:T(8,128)(2,1)S(1)} %get-tuple-element.10), channel_id=1, source_target_pairs={{0,6},{2,0},{4,2},{6,4},{1,7},{3,1},{5,3},{7,5},{8,14},{10,8},{12,... | collective-permute-start | bytes 172040 | tf_op jit(solution)/shard_map/ppermute | solution.py:17
  35.8 5.8 %collective-permute-start.17 = (bf16[8,3584]{1,0:T(8,128)(2,1)S(1)}, bf16[8,3584]{1,0:T(8,128)(2,1)S(1)}, u32[]{:S(2)}, u32[]{:S(2)}) collective-permute-start(bf16[8,3584]{1,0:T(8,128)(2,1)S(1)} %get-tuple-element.11), channel_id=1, source_target_pairs={{0,4},{2,6},{4,0},{6,2},{1,5},{3,7},{5,1},{7,3},{8,12},{10,14},{12... | collective-permute-start | bytes 172040 | tf_op jit(solution)/shard_map/ppermute | solution.py:17
  36.8 6.0 %collective-permute-start.18 = (bf16[8,3584]{1,0:T(8,128)(2,1)S(1)}, bf16[8,3584]{1,0:T(8,128)(2,1)S(1)}, u32[]{:S(2)}, u32[]{:S(2)}) collective-permute-start(bf16[8,3584]{1,0:T(8,128)(2,1)S(1)} %get-tuple-element.12), channel_id=1, source_target_pairs={{0,2},{2,4},{4,6},{6,0},{1,3},{3,5},{5,7},{7,1},{8,10},{10,12},{12... | collective-permute-start | bytes 172040 | tf_op jit(solution)/shard_map/ppermute | solution.py:17
where the time goes:
time: 43.6 us; the launch traced here: 43.4 us
  starting transfers between devices  24 us (55%)
  waiting for transfers between devices  12.8 us (29%)
  matrix products  4.09 us (9%)
  local copies, waits for them, and re-layouts  1.02 us (2%)
  other arithmetic  0.86 us (2%)
    ppermute x11, starting transfers between devices, shift(): lax.ppermute(value, axis, [(i, (i + by) % size) for i in range(size)])  18.3 us
    ppermute x11, waiting for transfers between devices, shift(): lax.ppermute(value, axis, [(i, (i + by) % size) for i in range(size)])  7.49 us
    ppermute x4, starting transfers between devices, shift_expert(): lax.ppermute(value, 'grp', [(i, (i + 2 * by) % groups) for i in range(gro...  5.2 us
    ppermute x4, waiting for transfers between devices, swap_half(): lax.ppermute(value, 'grp', [(i, i ^ 1) for i in range(lax.axis_size('grp'...  4.21 us
    dot_general x4, matrix products, partial_sums(): jnp.dot(rows, w, preferred_element_type=f32)  3.26 us
    ppermute x4, waiting for transfers between devices, shift_expert(): lax.ppermute(value, 'grp', [(i, (i + 2 * by) % groups) for i in range(gro...  1.14 us
    unnamed x16, local copies, waits for them, and re-layouts  0.94 us
  transfers between devices with their start and end apart: 19, of which 11 were waited for; matrix products, arithmetic and copies ran while one was open for 9% of the time, Pallas kernels for 1%

commit v1 on v0

--- a/solution.py
+++ b/solution.py
@@ -125,43 +125,41 @@
         sent = part.astype(bf16)
         return part, sent, [shift(sent, "ex", s) for s in range(1, n_ex)]
 
-    def partial_out(part, others, part_flops, kept_flops):
-        if part_flops:
-            part = after(part, flops=part_flops)
+    def partial_out(part, others, kept_flops, *earlier):
         for other in others:
             part = part + other.astype(f32)
         hidden = (jax.nn.silu(part[:, :inner]) * part[:, inner:]).astype(bf16)
         out = jnp.dot(hidden, w_down, preferred_element_type=f32)
         kept = out.shape[0] // 2
         swapped = swap_half(out[kept:].astype(bf16)).astype(f32)
-        if kept_flops:
-            out = after(out, flops=kept_flops)
-        return out[:kept] + swapped
+        kept_out = after(out, *earlier, flops=kept_flops)[:kept]
+        return out, kept_out + swapped
 
     held = copied(tokens)
     places = tuple(range(1, n_tp))
-    rest = joined([shift(tokens, "tp", t) for t in places])
-    far_own = [shift_expert(held, s) for s in others]
-    far_rest = [shift_expert(rest, s) for s in others]
-    near = joined([held, rest])
-    near_swapped = swap_half(near)
+    blocks = [held] + [shift(tokens, "tp", t) for t in places]
+    own_weight = weights_of(expert_ids, gate_levels, experts)
+    far = [[shift_expert(rows, s) for rows in blocks] for s in others]
+    near = joined(blocks)
+    near_swapped = swap_half(after(near, *(line[1] for line in far)))
     near = joined([near, near_swapped])
     near_part, near_sent, near_others = partial_sums(near)
-    far = joined([rows for own, other in zip(far_own, far_rest) for rows in (own, after(other, near_sent))])
+    far = joined([after(rows, near_sent) if i == n_tp - 1 else rows for line in far for i, rows in enumerate(line)])
     far_swapped = swap_half(far)
     far = joined([after(far, flops=3450000000), far_swapped])
     far_part, far_sent, far_others = partial_sums(far)
-    near_out = partial_out(near_part, [after(other, far_sent) for other in near_others], 3450000000, 3450000000)
-    far_out = partial_out(far_part, [after(other, near_out) for other in far_others], 0, 0).astype(bf16)
-    own_weight = weights_of(expert_ids, gate_levels, experts)
-    weights = [shift(own_weight, "tp", t) for t in places]
-    line, half = n_tp * count, 2 * count
-    back_b = [shift_expert(far_out[(s - 1) * line + half : s * line], -s) for s in others]
-    back_a = [shift_expert(far_out[(s - 1) * line : (s - 1) * line + half], -s) for s in others]
-    pieces_b = blended(near_out, half, weights[1:], back_b, [bf16] * (n_tp - 2))
-    own, piece_a = blended(near_out, 0, [own_weight, weights[0]], back_a, [f32, bf16])
+    near_whole, near_out = partial_out(near_part, [after(other, far_sent) for other in near_others], 3450000000)
+    weights = [own_weight] + [shift(after(own_weight, near_whole if i < 1 else near_out), "tp", t) for i, t in enumerate(places)]
+    _, far_out = partial_out(far_part, [after(other, near_out, *weights[9:]) for other in far_others], 3450000000, *weights[1:])
+    far_out = far_out.astype(bf16)
+    far_out = far_out.reshape(experts - 1, n_tp, count, width)
+    pieces = []
+    for i in reversed(range(n_tp)):
+        back = [shift_expert(far_out[s - 1, i], -s) for s in others]
+        pieces += blended(near_out, i * count, [weights[i]], back, [bf16 if i else f32])
+    own = pieces[-1]
     mixed = own
-    for t, piece in zip(places, [piece_a, *pieces_b]):
+    for t, piece in zip(reversed(places), pieces):
         mixed = mixed + shift(piece, "tp", -t).astype(f32)
     return mixed.astype(bf16)
 

time: 43.6 us -> 45.5 us (1.044)
  starting transfers between devices: 24 us -> 26.3 us
  matrix products: 4.09 us -> 2.59 us
  waiting for transfers between devices: 12.8 us -> 13.8 us
    ppermute x4 -> x8, starting transfers between devices: 5.2 us -> 9.26 us  [shift_expert(): lax.ppermute(value, 'grp', [(i, (i + 2 * by) % groups) for i in range(gro...]
    ppermute x11, waiting for transfers between devices: 7.49 us -> 9.28 us  [shift(): lax.ppermute(value, axis, [(i, (i + by) % size) for i in range(size)])]
    ppermute x11, starting transfers between devices: 18.3 us -> 16.7 us  [shift(): lax.ppermute(value, axis, [(i, (i + by) % size) for i in range(size)])]
    dot_general x4, matrix products: 3.26 us -> 1.76 us  [partial_sums(): jnp.dot(rows, w, preferred_element_type=f32)]
    ppermute x4, waiting for transfers between devices: 4.21 us -> 2.97 us  [swap_half(): lax.ppermute(value, 'grp', [(i, i ^ 1) for i in range(lax.axis_size('grp'...]
    ppermute x4 -> x8, waiting for transfers between devices: 1.14 us -> 1.57 us  [shift_expert(): lax.ppermute(value, 'grp', [(i, (i + 2 * by) % groups) for i in range(gro...]
    unnamed x16 -> x18, local copies, waits for them, and re-layouts: 0.94 us -> 0.91 us
  transfers between devices with their start and end apart: 19 -> 23, of which waited for: 11 -> 11; matrix products, arithmetic and copies ran while one was open for 9% -> 6% of each run, Pallas kernels for 1% -> 1%
where the time goes in v1:
time: 45.5 us; the launch traced here: 45.3 us
  starting transfers between devices  26.3 us (58%)
  waiting for transfers between devices  13.8 us (30%)
  matrix products  2.59 us (6%)
  local copies, waits for them, and re-layouts  0.99 us (2%)
  other arithmetic  0.83 us (2%)
  Pallas kernels  0.54 us (1%)
    ppermute x11, starting transfers between devices, shift(): lax.ppermute(value, axis, [(i, (i + by) % size) for i in range(size)])  16.7 us
    ppermute x11, waiting for transfers between devices, shift(): lax.ppermute(value, axis, [(i, (i + by) % size) for i in range(size)])  9.28 us
    ppermute x8, starting transfers between devices, shift_expert(): lax.ppermute(value, 'grp', [(i, (i + 2 * by) % groups) for i in range(gro...  9.26 us
    ppermute x4, waiting for transfers between devices, swap_half(): lax.ppermute(value, 'grp', [(i, i ^ 1) for i in range(lax.axis_size('grp'...  2.97 us
    dot_general x4, matrix products, partial_sums(): jnp.dot(rows, w, preferred_element_type=f32)  1.76 us
    ppermute x8, waiting for transfers between devices, shift_expert(): lax.ppermute(value, 'grp', [(i, (i + 2 * by) % groups) for i in range(gro...  1.57 us
  transfers between devices with their start and end apart: 23, of which 11 were waited for; matrix products, arithmetic and copies ran while one was open for 6% of the time, Pallas kernels for 1%

profile of v1, /device:TPU:0, one launch (start us, length us, event | category | flops | bytes accessed | tf_op | source)
XLA Modules:
  0.0 45.3 jit_solution(13045280163850830274)
XLA Ops:
  0.0 0.0 copy-start
  0.0 3.0 %collective-permute-start = (bf16[8,3584]{1,0:T(8,128)(2,1)}, bf16[8,3584]{1,0:T(8,128)(2,1)S(1)}, u32[]{:S(2)}, u32[]{:S(2)}) collective-permute-start(bf16[8,3584]{1,0:T(8,128)(2,1)} %from_ref.1), channel_id=1, source_target_pairs={{0,2},{2,4},{4,6},{6,0},{1,3},{3,5},{5,7},{7,1},{8,10},{10,12},{12... | collective-permute-start | bytes 172040 | tf_op jit(solution)/shard_map/ppermute | solution.py:17
  3.0 2.1 %collective-permute-start.2 = (bf16[8,3584]{1,0:T(8,128)(2,1)}, bf16[8,3584]{1,0:T(8,128)(2,1)S(1)}, u32[]{:S(2)}, u32[]{:S(2)}) collective-permute-start(bf16[8,3584]{1,0:T(8,128)(2,1)} %from_ref.1), channel_id=1, source_target_pairs={{0,6},{2,0},{4,2},{6,4},{1,7},{3,1},{5,3},{7,5},{8,14},{10,8},{12,... | collective-permute-start | bytes 172040 | tf_op jit(solution)/shard_map/ppermute | solution.py:17
  5.1 1.0 %collective-permute-start.1 = (bf16[8,3584]{1,0:T(8,128)(2,1)}, bf16[8,3584]{1,0:T(8,128)(2,1)S(1)}, u32[]{:S(2)}, u32[]{:S(2)}) collective-permute-start(bf16[8,3584]{1,0:T(8,128)(2,1)} %from_ref.1), channel_id=1, source_target_pairs={{0,4},{2,6},{4,0},{6,2},{1,5},{3,7},{5,1},{7,3},{8,12},{10,14},{12... | collective-permute-start | bytes 172040 | tf_op jit(solution)/shard_map/ppermute | solution.py:17
  6.1 0.9 %copy-done.1 = bf16[8,3584]{1,0:T(8,128)(2,1)S(1)} copy-done((bf16[8,3584]{1,0:T(8,128)(2,1)S(1)}, bf16[8,3584]{1,0:T(8,128)(2,1)}, u32[]{:S(2)}) %copy-start.1) | copy-done | bytes 57368
  6.9 1.5 %collective-permute-start.6 = (bf16[8,3584]{1,0:T(8,128)(2,1)S(1)}, bf16[8,3584]{1,0:T(8,128)(2,1)S(1)}, u32[]{:S(2)}, u32[]{:S(2)}) collective-permute-start(bf16[8,3584]{1,0:T(8,128)(2,1)S(1)} %shard_map.64), channel_id=1, source_target_pairs={{0,16},{8,24},{16,0},{24,8},{1,17},{9,25},{17,1},{25,9},{2,18},{10... | collective-permute-start | bytes 172040 | tf_op jit(solution)/shard_map/ppermute | solution.py:22
  8.4 0.0 collective-permute-done
  8.4 1.0 %collective-permute-start.3 = (bf16[8,3584]{1,0:T(8,128)(2,1)S(1)}, bf16[8,3584]{1,0:T(8,128)(2,1)S(1)}, u32[]{:S(2)}, u32[]{:S(2)}) collective-permute-start(bf16[8,3584]{1,0:T(8,128)(2,1)S(1)} %collective-permute-done), channel_id=1, source_target_pairs={{0,16},{8,24},{16,0},{24,8},{1,17},{9,25},{17,1},{25,9},{2,18},{10... | collective-permute-start | bytes 172040 | tf_op jit(solution)/shard_map/ppermute | solution.py:22
  9.4 0.0 collective-permute-done.2
  9.4 1.1 %collective-permute-start.8 = (bf16[8,3584]{1,0:T(8,128)(2,1)S(1)}, bf16[8,3584]{1,0:T(8,128)(2,1)S(1)}, u32[]{:S(2)}, u32[]{:S(2)}) collective-permute-start(bf16[8,3584]{1,0:T(8,128)(2,1)S(1)} %collective-permute-done.2), channel_id=1, source_target_pairs={{0,16},{8,24},{16,0},{24,8},{1,17},{9,25},{17,1},{25,9},{2,18},{10... | collective-permute-start | bytes 172040 | tf_op jit(solution)/shard_map/ppermute | solution.py:22
  10.5 0.4 collective-permute-done.1
  10.9 1.6 %collective-permute-start.7 = (bf16[8,3584]{1,0:T(8,128)(2,1)S(1)}, bf16[8,3584]{1,0:T(8,128)(2,1)S(1)}, u32[]{:S(2)}, u32[]{:S(2)}) collective-permute-start(bf16[8,3584]{1,0:T(8,128)(2,1)S(1)} %collective-permute-done.1), channel_id=1, source_target_pairs={{0,16},{8,24},{16,0},{24,8},{1,17},{9,25},{17,1},{25,9},{2,18},{10... | collective-permute-start | bytes 172040 | tf_op jit(solution)/shard_map/ppermute | solution.py:22
  12.5 0.0 copy-start.5
  12.5 0.2 collective-permute-done.3.refs_1_
  12.7 0.0 collective-permute-start.4
  12.7 1.5 %collective-permute-done.4 = bf16[32,3584]{1,0:T(8,128)(2,1)S(1)} collective-permute-done((bf16[32,3584]{1,0:T(8,128)(2,1)S(1)}, bf16[32,3584]{1,0:T(8,128)(2,1)S(1)}, u32[]{:S(2)}, u32[]{:S(2)}) %collective-permute-start.4) | collective-permute-done | bytes 229408 | tf_op jit(solution)/shard_map/ppermute | solution.py:26
  14.2 0.0 copy-done.4
  14.2 0.4 fusion.6
  14.6 0.0 copy-start.2
  14.7 0.0 copy-start.3
  14.7 0.4 fusion.10
  15.1 0.0 collective-permute-done.8.refs_0_
  15.1 0.0 collective-permute-done.6
  15.2 0.0 collective-permute-done.7
  15.2 0.2 collective-permute-start.9
  15.4 0.1 shard_map.70.refs_0_
  15.5 1.6 %collective-permute-start.5 = (bf16[64,512]{1,0:T(8,128)(2,1)S(1)}, bf16[64,512]{1,0:T(8,128)(2,1)S(1)}, u32[]{:S(2)}, u32[]{:S(2)}) collective-permute-start(bf16[64,512]{1,0:T(8,128)(2,1)S(1)} %fusion.15.refs_1_), channel_id=1, source_target_pairs={{0,1},{1,0},{2,3},{3,2},{4,5},{5,4},{6,7},{7,6},{8,9},{9,8},{10,11... | collective-permute-start | bytes 196616 | tf_op jit(solution)/shard_map/ppermute | solution.py:17
  17.1 0.0 collective-permute-done.9
  17.1 0.4 fusion.4
  17.5 0.4 fusion.8
  18.0 1.2 %collective-permute-start.11 = (bf16[64,512]{1,0:T(8,128)(2,1)S(1)}, bf16[64,512]{1,0:T(8,128)(2,1)S(1)}, u32[]{:S(2)}, u32[]{:S(2)}) collective-permute-start(bf16[64,512]{1,0:T(8,128)(2,1)S(1)} %fusion.14.refs_1_), channel_id=1, source_target_pairs={{0,1},{1,0},{2,3},{3,2},{4,5},{5,4},{6,7},{7,6},{8,9},{9,8},{10,11... | collective-permute-start | bytes 196616 | tf_op jit(solution)/shard_map/ppermute | solution.py:17
  19.2 0.7 %collective-permute-done.5.refs_0_ = bf16[64,512]{1,0:T(8,128)(2,1)S(1)} collective-permute-done((bf16[64,512]{1,0:T(8,128)(2,1)S(1)}, bf16[64,512]{1,0:T(8,128)(2,1)S(1)}, u32[]{:S(2)}, u32[]{:S(2)}) %collective-permute-start.5) | collective-permute-done | bytes 65568 | tf_op jit(solution)/shard_map/ppermute | solution.py:17
  20.0 0.4 fusion.2.refs_0_.refs_1_
  20.4 1.8 %collective-permute-start.12 = (f32[8,128]{1,0:T(8,128)S(1)}, f32[8,128]{1,0:T(8,128)S(1)}, u32[]{:S(2)}, u32[]{:S(2)}) collective-permute-start(f32[8,128]{1,0:T(8,128)S(1)} %shard_map.72), channel_id=1, source_target_pairs={{0,2},{2,4},{4,6},{6,0},{1,3},{3,5},{5,7},{7,1},{8,10},{10,12},{12... | collective-permute-start | bytes 12296 | tf_op jit(solution)/shard_map/ppermute | solution.py:17
  22.2 0.0 collective-permute-start.10
  22.3 1.5 %collective-permute-done.10 = bf16[32,3584]{1,0:T(8,128)(2,1)S(1)} collective-permute-done((bf16[32,3584]{1,0:T(8,128)(2,1)S(1)}, bf16[32,3584]{1,0:T(8,128)(2,1)S(1)}, u32[]{:S(2)}, u32[]{:S(2)}) %collective-permute-start.10) | collective-permute-done | bytes 229408 | tf_op jit(solution)/shard_map/ppermute | solution.py:26
  23.8 2.1 %collective-permute-start.14 = (f32[8,128]{1,0:T(8,128)S(1)}, f32[8,128]{1,0:T(8,128)S(1)}, u32[]{:S(2)}, u32[]{:S(2)}) collective-permute-start(f32[8,128]{1,0:T(8,128)S(1)} %shard_map.73), channel_id=1, source_target_pairs={{0,6},{2,0},{4,2},{6,4},{1,7},{3,1},{5,3},{7,5},{8,14},{10,8},{12,... | collective-permute-start | bytes 12296 | tf_op jit(solution)/shard_map/ppermute | solution.py:17
  25.9 0.7 %collective-permute-start.13 = (f32[8,128]{1,0:T(8,128)S(1)}, f32[8,128]{1,0:T(8,128)S(1)}, u32[]{:S(2)}, u32[]{:S(2)}) collective-permute-start(f32[8,128]{1,0:T(8,128)S(1)} %shard_map.73), channel_id=1, source_target_pairs={{0,4},{2,6},{4,0},{6,2},{1,5},{3,7},{5,1},{7,3},{8,12},{10,14},{12... | collective-permute-start | bytes 12296 | tf_op jit(solution)/shard_map/ppermute | solution.py:17
  26.5 0.0 collective-permute-done.11.refs_0_
  26.6 0.4 fusion.refs_0_
  27.0 0.1 collective-permute-start.15
  27.1 0.0 collective-permute-done.12.refs_1_.refs_0_
  27.1 0.3 collective-permute-done.14.refs_3_.refs_0_
  27.5 2.9 %collective-permute-done.13.refs_2_.refs_0_ = f32[8,128]{1,0:T(8,128)S(1)} collective-permute-done((f32[8,128]{1,0:T(8,128)S(1)}, f32[8,128]{1,0:T(8,128)S(1)}, u32[]{:S(2)}, u32[]{:S(2)}) %collective-permute-start.13) | collective-permute-done | bytes 4128 | tf_op jit(solution)/shard_map/ppermute | solution.py:17
  30.4 0.0 collective-permute-done.15
  30.5 1.5 %collective-permute-start.17 = (bf16[8,3584]{1,0:T(8,128)(2,1)S(1)}, bf16[8,3584]{1,0:T(8,128)(2,1)S(1)}, u32[]{:S(2)}, u32[]{:S(2)}) collective-permute-start(bf16[8,3584]{1,0:T(8,128)(2,1)S(1)} %get-tuple-element.5), channel_id=1, source_target_pairs={{0,16},{8,24},{16,0},{24,8},{1,17},{9,25},{17,1},{25,9},{2,18},{10... | collective-permute-start | bytes 172040 | tf_op jit(solution)/shard_map/ppermute | solution.py:22
  32.0 0.6 %collective-permute-start.21 = (bf16[8,3584]{1,0:T(8,128)(2,1)S(1)}, bf16[8,3584]{1,0:T(8,128)(2,1)S(1)}, u32[]{:S(2)}, u32[]{:S(2)}) collective-permute-start(bf16[8,3584]{1,0:T(8,128)(2,1)S(1)} %get-tuple-element.6), channel_id=1, source_target_pairs={{0,16},{8,24},{16,0},{24,8},{1,17},{9,25},{17,1},{25,9},{2,18},{10... | collective-permute-start | bytes 172040 | tf_op jit(solution)/shard_map/ppermute | solution.py:22
  32.6 1.5 %collective-permute-start.19 = (bf16[8,3584]{1,0:T(8,128)(2,1)S(1)}, bf16[8,3584]{1,0:T(8,128)(2,1)S(1)}, u32[]{:S(2)}, u32[]{:S(2)}) collective-permute-start(bf16[8,3584]{1,0:T(8,128)(2,1)S(1)} %get-tuple-element.7), channel_id=1, source_target_pairs={{0,16},{8,24},{16,0},{24,8},{1,17},{9,25},{17,1},{25,9},{2,18},{10... | collective-permute-start | bytes 172040 | tf_op jit(solution)/shard_map/ppermute | solution.py:22
  34.0 0.6 %collective-permute-start.16 = (bf16[8,3584]{1,0:T(8,128)(2,1)S(1)}, bf16[8,3584]{1,0:T(8,128)(2,1)S(1)}, u32[]{:S(2)}, u32[]{:S(2)}) collective-permute-start(bf16[8,3584]{1,0:T(8,128)(2,1)S(1)} %get-tuple-element.8), channel_id=1, source_target_pairs={{0,16},{8,24},{16,0},{24,8},{1,17},{9,25},{17,1},{25,9},{2,18},{10... | collective-permute-start | bytes 172040 | tf_op jit(solution)/shard_map/ppermute | solution.py:22
  34.6 0.6 %collective-permute-done.17.refs_1_ = bf16[8,3584]{1,0:T(8,128)(2,1)S(1)} collective-permute-done((bf16[8,3584]{1,0:T(8,128)(2,1)S(1)}, bf16[8,3584]{1,0:T(8,128)(2,1)S(1)}, u32[]{:S(2)}, u32[]{:S(2)}) %collective-permute-start.17) | collective-permute-done | bytes 57376 | tf_op jit(solution)/shard_map/ppermute | solution.py:22
  35.2 0.1 shard_map.76
  35.3 0.1 collective-permute-start.18
  35.4 0.8 %collective-permute-done.21.refs_1_ = bf16[8,3584]{1,0:T(8,128)(2,1)S(1)} collective-permute-done((bf16[8,3584]{1,0:T(8,128)(2,1)S(1)}, bf16[8,3584]{1,0:T(8,128)(2,1)S(1)}, u32[]{:S(2)}, u32[]{:S(2)}) %collective-permute-start.21) | collective-permute-done | bytes 57376 | tf_op jit(solution)/shard_map/ppermute | solution.py:22
  36.2 0.1 shard_map.78
  36.3 3.1 %collective-permute-start.22 = (bf16[8,3584]{1,0:T(8,128)(2,1)S(1)}, bf16[8,3584]{1,0:T(8,128)(2,1)S(1)}, u32[]{:S(2)}, u32[]{:S(2)}) collective-permute-start(bf16[8,3584]{1,0:T(8,128)(2,1)S(1)} %shard_map.78), channel_id=1, source_target_pairs={{0,6},{2,0},{4,2},{6,4},{1,7},{3,1},{5,3},{7,5},{8,14},{10,8},{12,... | collective-permute-start | bytes 172040 | tf_op jit(solution)/shard_map/ppermute | solution.py:17
  39.4 0.0 collective-permute-done.19.refs_1_
  39.4 0.1 shard_map.77
  39.5 0.1 collective-permute-start.20
  39.6 0.0 collective-permute-done.16.refs_1_
  39.6 0.1 shard_map.75
  39.7 1.7 %collective-permute-done.18 = bf16[8,3584]{1,0:T(8,128)(2,1)S(1)} collective-permute-done((bf16[8,3584]{1,0:T(8,128)(2,1)S(1)}, bf16[8,3584]{1,0:T(8,128)(2,1)S(1)}, u32[]{:S(2)}, u32[]{:S(2)}) %collective-permute-start.18) | collective-permute-done | bytes 57376 | tf_op jit(solution)/shard_map/ppermute | solution.py:17
  41.5 0.0 collective-permute-done.22
  41.5 3.2 %collective-permute-done.20 = bf16[8,3584]{1,0:T(8,128)(2,1)S(1)} collective-permute-done((bf16[8,3584]{1,0:T(8,128)(2,1)S(1)}, bf16[8,3584]{1,0:T(8,128)(2,1)S(1)}, u32[]{:S(2)}, u32[]{:S(2)}) %collective-permute-start.20) | collective-permute-done | bytes 57376 | tf_op jit(solution)/shard_map/ppermute | solution.py:17
  44.6 0.7 %add_convert_fusion = bf16[8,3584]{1,0:T(8,128)(2,1)} fusion(bf16[8,3584]{1,0:T(8,128)(2,1)S(1)} %collective-permute-done.22, bf16[8,3584]{1,0:T(8,128)(2,1)S(1)} %collective-permute-done.20, f32[8,3584]{1,0:T(8,128)S(1)} %shard_map.75, bf16[8,3584]{1,0:T(8,128)(2,1)S(1)} %collective-permute-done.18), kind=kLoop, calls=%fused_computation.25 | loop fusion | flops 200704 | bytes 344064 | tf_op jit(solution)/shard_map/convert_element_type | solution.py:164
  (34 shorter events, 0.3 us)
Async XLA Ops:
  0.0 19.9 %copy-start = (bf16[1,256,3584]{2,1,0:T(8,128)(2,1)S(1)}, bf16[1,256,3584]{2,1,0:T(8,128)(2,1)}, u32[]{:S(2)}) copy-start(bf16[1,256,3584]{2,1,0:T(8,128)(2,1)} %param.11) | copy-start | bytes 5505028
  0.0 8.4 %collective-permute-start = (bf16[8,3584]{1,0:T(8,128)(2,1)}, bf16[8,3584]{1,0:T(8,128)(2,1)S(1)}, u32[]{:S(2)}, u32[]{:S(2)}) collective-permute-start(bf16[8,3584]{1,0:T(8,128)(2,1)} %from_ref.1), channel_id=1, source_target_pairs={{0,2},{2,4},{4,6},{6,0},{1,3},{3,5},{5,7},{7,1},{8,10},{10,12},{12... | collective-permute-start | bytes 172040 | tf_op jit(solution)/shard_map/ppermute | solution.py:17
  3.0 6.4 %collective-permute-start.2 = (bf16[8,3584]{1,0:T(8,128)(2,1)}, bf16[8,3584]{1,0:T(8,128)(2,1)S(1)}, u32[]{:S(2)}, u32[]{:S(2)}) collective-permute-start(bf16[8,3584]{1,0:T(8,128)(2,1)} %from_ref.1), channel_id=1, source_target_pairs={{0,6},{2,0},{4,2},{6,4},{1,7},{3,1},{5,3},{7,5},{8,14},{10,8},{12,... | collective-permute-start | bytes 172040 | tf_op jit(solution)/shard_map/ppermute | solution.py:17
  5.1 5.8 %collective-permute-start.1 = (bf16[8,3584]{1,0:T(8,128)(2,1)}, bf16[8,3584]{1,0:T(8,128)(2,1)S(1)}, u32[]{:S(2)}, u32[]{:S(2)}) collective-permute-start(bf16[8,3584]{1,0:T(8,128)(2,1)} %from_ref.1), channel_id=1, source_target_pairs={{0,4},{2,6},{4,0},{6,2},{1,5},{3,7},{5,1},{7,3},{8,12},{10,14},{12... | collective-permute-start | bytes 172040 | tf_op jit(solution)/shard_map/ppermute | solution.py:17
  6.1 0.9 %copy-start.1 = (bf16[8,3584]{1,0:T(8,128)(2,1)S(1)}, bf16[8,3584]{1,0:T(8,128)(2,1)}, u32[]{:S(2)}) copy-start(bf16[8,3584]{1,0:T(8,128)(2,1)} %from_ref.1) | copy-start | bytes 172036
  6.9 7.3 %copy-start.4 = (bf16[1,3584,256]{2,1,0:T(8,128)(2,1)S(1)}, bf16[1,3584,256]{2,1,0:T(8,128)(2,1)}, u32[]{:S(2)}) copy-start(bf16[1,3584,256]{2,1,0:T(8,128)(2,1)} %param.10) | copy-start | bytes 5505028
  6.9 8.2 %collective-permute-start.6 = (bf16[8,3584]{1,0:T(8,128)(2,1)S(1)}, bf16[8,3584]{1,0:T(8,128)(2,1)S(1)}, u32[]{:S(2)}, u32[]{:S(2)}) collective-permute-start(bf16[8,3584]{1,0:T(8,128)(2,1)S(1)} %shard_map.64), channel_id=1, source_target_pairs={{0,16},{8,24},{16,0},{24,8},{1,17},{9,25},{17,1},{25,9},{2,18},{10... | collective-permute-start | bytes 172040 | tf_op jit(solution)/shard_map/ppermute | solution.py:22
  8.4 4.2 %collective-permute-start.3 = (bf16[8,3584]{1,0:T(8,128)(2,1)S(1)}, bf16[8,3584]{1,0:T(8,128)(2,1)S(1)}, u32[]{:S(2)}, u32[]{:S(2)}) collective-permute-start(bf16[8,3584]{1,0:T(8,128)(2,1)S(1)} %collective-permute-done), channel_id=1, source_target_pairs={{0,16},{8,24},{16,0},{24,8},{1,17},{9,25},{17,1},{25,9},{2,18},{10... | collective-permute-start | bytes 172040 | tf_op jit(solution)/shard_map/ppermute | solution.py:22
  9.4 5.7 %collective-permute-start.8 = (bf16[8,3584]{1,0:T(8,128)(2,1)S(1)}, bf16[8,3584]{1,0:T(8,128)(2,1)S(1)}, u32[]{:S(2)}, u32[]{:S(2)}) collective-permute-start(bf16[8,3584]{1,0:T(8,128)(2,1)S(1)} %collective-permute-done.2), channel_id=1, source_target_pairs={{0,16},{8,24},{16,0},{24,8},{1,17},{9,25},{17,1},{25,9},{2,18},{10... | collective-permute-start | bytes 172040 | tf_op jit(solution)/shard_map/ppermute | solution.py:22
  10.9 4.3 %collective-permute-start.7 = (bf16[8,3584]{1,0:T(8,128)(2,1)S(1)}, bf16[8,3584]{1,0:T(8,128)(2,1)S(1)}, u32[]{:S(2)}, u32[]{:S(2)}) collective-permute-start(bf16[8,3584]{1,0:T(8,128)(2,1)S(1)} %collective-permute-done.1), channel_id=1, source_target_pairs={{0,16},{8,24},{16,0},{24,8},{1,17},{9,25},{17,1},{25,9},{2,18},{10... | collective-permute-start | bytes 172040 | tf_op jit(solution)/shard_map/ppermute | solution.py:22
  12.5 2.2 %copy-start.5 = (bf16[1,3584,256]{2,1,0:T(8,128)(2,1)S(1)}, bf16[1,3584,256]{2,1,0:T(8,128)(2,1)}, u32[]{:S(2)}) copy-start(bf16[1,3584,256]{2,1,0:T(8,128)(2,1)} %param.9) | copy-start | bytes 5505028
  12.7 1.5 %collective-permute-start.4 = (bf16[32,3584]{1,0:T(8,128)(2,1)S(1)}, bf16[32,3584]{1,0:T(8,128)(2,1)S(1)}, u32[]{:S(2)}, u32[]{:S(2)}) collective-permute-start(bf16[32,3584]{1,0:T(8,128)(2,1)S(1)} %shard_map.65), channel_id=1, source_target_pairs={{0,8},{8,0},{16,24},{24,16},{1,9},{9,1},{17,25},{25,17},{2,10},{10... | collective-permute-start | bytes 688136 | tf_op jit(solution)/shard_map/ppermute | solution.py:26
  14.6 0.8 %copy-start.2 = (s32[8,1]{0,1:T(1,128)S(1)}, s32[8,1]{0,1:T(1,128)}, u32[]{:S(2)}) copy-start(s32[8,1]{0,1:T(1,128)} %param.7) | copy-start | bytes 100
  14.7 0.7 %copy-start.3 = (s32[8,1]{0,1:T(1,128)S(1)}, s32[8,1]{0,1:T(1,128)}, u32[]{:S(2)}) copy-start(s32[8,1]{0,1:T(1,128)} %param.8) | copy-start | bytes 100
  15.2 1.9 %collective-permute-start.9 = (bf16[32,3584]{1,0:T(8,128)(2,1)S(1)}, bf16[32,3584]{1,0:T(8,128)(2,1)S(1)}, u32[]{:S(2)}, u32[]{:S(2)}) collective-permute-start(bf16[32,3584]{1,0:T(8,128)(2,1)S(1)} %pad_maximum_fusion.4.refs_0_), channel_id=1, source_target_pairs={{0,8},{8,0},{16,24},{24,16},{1,9},{9,1},{17,25},{25,17},{2,10},{10... | collective-permute-start | bytes 688136 | tf_op jit(solution)/shard_map/ppermute | solution.py:26
  15.5 4.4 %collective-permute-start.5 = (bf16[64,512]{1,0:T(8,128)(2,1)S(1)}, bf16[64,512]{1,0:T(8,128)(2,1)S(1)}, u32[]{:S(2)}, u32[]{:S(2)}) collective-permute-start(bf16[64,512]{1,0:T(8,128)(2,1)S(1)} %fusion.15.refs_1_), channel_id=1, source_target_pairs={{0,1},{1,0},{2,3},{3,2},{4,5},{5,4},{6,7},{7,6},{8,9},{9,8},{10,11... | collective-permute-start | bytes 196616 | tf_op jit(solution)/shard_map/ppermute | solution.py:17
  18.0 8.5 %collective-permute-start.11 = (bf16[64,512]{1,0:T(8,128)(2,1)S(1)}, bf16[64,512]{1,0:T(8,128)(2,1)S(1)}, u32[]{:S(2)}, u32[]{:S(2)}) collective-permute-start(bf16[64,512]{1,0:T(8,128)(2,1)S(1)} %fusion.14.refs_1_), channel_id=1, source_target_pairs={{0,1},{1,0},{2,3},{3,2},{4,5},{5,4},{6,7},{7,6},{8,9},{9,8},{10,11... | collective-permute-start | bytes 196616 | tf_op jit(solution)/shard_map/ppermute | solution.py:17
  20.4 6.7 %collective-permute-start.12 = (f32[8,128]{1,0:T(8,128)S(1)}, f32[8,128]{1,0:T(8,128)S(1)}, u32[]{:S(2)}, u32[]{:S(2)}) collective-permute-start(f32[8,128]{1,0:T(8,128)S(1)} %shard_map.72), channel_id=1, source_target_pairs={{0,2},{2,4},{4,6},{6,0},{1,3},{3,5},{5,7},{7,1},{8,10},{10,12},{12... | collective-permute-start | bytes 12296 | tf_op jit(solution)/shard_map/ppermute | solution.py:17
  22.2 1.5 %collective-permute-start.10 = (bf16[32,3584]{1,0:T(8,128)(2,1)S(1)}, bf16[32,3584]{1,0:T(8,128)(2,1)S(1)}, u32[]{:S(2)}, u32[]{:S(2)}) collective-permute-start(bf16[32,3584]{1,0:T(8,128)(2,1)S(1)} %slice.87), channel_id=1, source_target_pairs={{0,8},{8,0},{16,24},{24,16},{1,9},{9,1},{17,25},{25,17},{2,10},{10... | collective-permute-start | bytes 688136 | tf_op jit(solution)/shard_map/ppermute | solution.py:26
  23.8 3.7 %collective-permute-start.14 = (f32[8,128]{1,0:T(8,128)S(1)}, f32[8,128]{1,0:T(8,128)S(1)}, u32[]{:S(2)}, u32[]{:S(2)}) collective-permute-start(f32[8,128]{1,0:T(8,128)S(1)} %shard_map.73), channel_id=1, source_target_pairs={{0,6},{2,0},{4,2},{6,4},{1,7},{3,1},{5,3},{7,5},{8,14},{10,8},{12,... | collective-permute-start | bytes 12296 | tf_op jit(solution)/shard_map/ppermute | solution.py:17
  25.9 4.5 %collective-permute-start.13 = (f32[8,128]{1,0:T(8,128)S(1)}, f32[8,128]{1,0:T(8,128)S(1)}, u32[]{:S(2)}, u32[]{:S(2)}) collective-permute-start(f32[8,128]{1,0:T(8,128)S(1)} %shard_map.73), channel_id=1, source_target_pairs={{0,4},{2,6},{4,0},{6,2},{1,5},{3,7},{5,1},{7,3},{8,12},{10,14},{12... | collective-permute-start | bytes 12296 | tf_op jit(solution)/shard_map/ppermute | solution.py:17
  27.0 3.4 %collective-permute-start.15 = (bf16[32,3584]{1,0:T(8,128)(2,1)S(1)}, bf16[32,3584]{1,0:T(8,128)(2,1)S(1)}, u32[]{:S(2)}, u32[]{:S(2)}) collective-permute-start(bf16[32,3584]{1,0:T(8,128)(2,1)S(1)} %slice.86), channel_id=1, source_target_pairs={{0,8},{8,0},{16,24},{24,16},{1,9},{9,1},{17,25},{25,17},{2,10},{10... | collective-permute-start | bytes 688136 | tf_op jit(solution)/shard_map/ppermute | solution.py:26
  30.5 4.8 %collective-permute-start.17 = (bf16[8,3584]{1,0:T(8,128)(2,1)S(1)}, bf16[8,3584]{1,0:T(8,128)(2,1)S(1)}, u32[]{:S(2)}, u32[]{:S(2)}) collective-permute-start(bf16[8,3584]{1,0:T(8,128)(2,1)S(1)} %get-tuple-element.5), channel_id=1, source_target_pairs={{0,16},{8,24},{16,0},{24,8},{1,17},{9,25},{17,1},{25,9},{2,18},{10... | collective-permute-start | bytes 172040 | tf_op jit(solution)/shard_map/ppermute | solution.py:22
  32.0 4.2 %collective-permute-start.21 = (bf16[8,3584]{1,0:T(8,128)(2,1)S(1)}, bf16[8,3584]{1,0:T(8,128)(2,1)S(1)}, u32[]{:S(2)}, u32[]{:S(2)}) collective-permute-start(bf16[8,3584]{1,0:T(8,128)(2,1)S(1)} %get-tuple-element.6), channel_id=1, source_target_pairs={{0,16},{8,24},{16,0},{24,8},{1,17},{9,25},{17,1},{25,9},{2,18},{10... | collective-permute-start | bytes 172040 | tf_op jit(solution)/shard_map/ppermute | solution.py:22
  32.6 6.8 %collective-permute-start.19 = (bf16[8,3584]{1,0:T(8,128)(2,1)S(1)}, bf16[8,3584]{1,0:T(8,128)(2,1)S(1)}, u32[]{:S(2)}, u32[]{:S(2)}) collective-permute-start(bf16[8,3584]{1,0:T(8,128)(2,1)S(1)} %get-tuple-element.7), channel_id=1, source_target_pairs={{0,16},{8,24},{16,0},{24,8},{1,17},{9,25},{17,1},{25,9},{2,18},{10... | collective-permute-start | bytes 172040 | tf_op jit(solution)/shard_map/ppermute | solution.py:22
  34.0 5.6 %collective-permute-start.16 = (bf16[8,3584]{1,0:T(8,128)(2,1)S(1)}, bf16[8,3584]{1,0:T(8,128)(2,1)S(1)}, u32[]{:S(2)}, u32[]{:S(2)}) collective-permute-start(bf16[8,3584]{1,0:T(8,128)(2,1)S(1)} %get-tuple-element.8), channel_id=1, source_target_pairs={{0,16},{8,24},{16,0},{24,8},{1,17},{9,25},{17,1},{25,9},{2,18},{10... | collective-permute-start | bytes 172040 | tf_op jit(solution)/shard_map/ppermute | solution.py:22
  35.3 6.1 %collective-permute-start.18 = (bf16[8,3584]{1,0:T(8,128)(2,1)S(1)}, bf16[8,3584]{1,0:T(8,128)(2,1)S(1)}, u32[]{:S(2)}, u32[]{:S(2)}) collective-permute-start(bf16[8,3584]{1,0:T(8,128)(2,1)S(1)} %shard_map.76), channel_id=1, source_target_pairs={{0,2},{2,4},{4,6},{6,0},{1,3},{3,5},{5,7},{7,1},{8,10},{10,12},{12... | collective-permute-start | bytes 172040 | tf_op jit(solution)/shard_map/ppermute | solution.py:17
  36.3 5.2 %collective-permute-start.22 = (bf16[8,3584]{1,0:T(8,128)(2,1)S(1)}, bf16[8,3584]{1,0:T(8,128)(2,1)S(1)}, u32[]{:S(2)}, u32[]{:S(2)}) collective-permute-start(bf16[8,3584]{1,0:T(8,128)(2,1)S(1)} %shard_map.78), channel_id=1, source_target_pairs={{0,6},{2,0},{4,2},{6,4},{1,7},{3,1},{5,3},{7,5},{8,14},{10,8},{12,... | collective-permute-start | bytes 172040 | tf_op jit(solution)/shard_map/ppermute | solution.py:17
  39.5 5.1 %collective-permute-start.20 = (bf16[8,3584]{1,0:T(8,128)(2,1)S(1)}, bf16[8,3584]{1,0:T(8,128)(2,1)S(1)}, u32[]{:S(2)}, u32[]{:S(2)}) collective-permute-start(bf16[8,3584]{1,0:T(8,128)(2,1)S(1)} %shard_map.77), channel_id=1, source_target_pairs={{0,4},{2,6},{4,0},{6,2},{1,5},{3,7},{5,1},{7,3},{8,12},{10,14},{12... | collective-permute-start | bytes 172040 | tf_op jit(solution)/shard_map/ppermute | solution.py:17
